TPU v7x, 128 devices: a whole 4x4x4 slice. The times are simulated.
128 devices in a mesh: region: 32 (over y, x, core), band: 4 (over z).
Axes of the slice: x: 4, y: 4, z: 4, core: 2. Of those that a mesh axis runs over, the one named last changes fastest.
Arguments:
- anomalies: bfloat16 [2097152, 128], P(('region', 'band')), may hold values from -28 to 28
- operator: bfloat16 [2048, 4, 128, 128], P(('region', 'band')), may hold values from -0.0014648438 to 0.0014648438
- local_tile_index: int32 [2048, 4], P(('region', 'band')), may hold values from 0 to 127
- err_std: float32 [262144], P(('region', 'band')), may hold values from 3 to 58
- err_corr: float32 [262144], P(('region', 'band')), may hold values from -1 to 1
Outputs:
- whitened: float32 [262144, 128], P(('region', 'band'))
- updated: bfloat16 [2097152, 128], P(('region', 'band'))
Inputs may be any that keep to these rules, and one draw needn't show every extreme that they name: `local_tile_index`: entry [j, k] names a tile of the device that lies k places further along band, cyclically, in the region of the device that holds block j.
All inputs are finite; a program needn't handle non-finite values.
Results may differ from a plain program's by a relative error of at most 0.0043.
The roundings to bfloat16 on the way count: a program that leaves them out, or rounds other values in their place, can miss the bound.
Values may be sent and summed in bfloat16 or wider, within the bound.
A program may use at most 64 MiB of HBM per device.

v0:
```python
import math

import jax
import jax.numpy as jnp
from jax import lax
from jax.sharding import Mesh
from jax.sharding import PartitionSpec as P

REGION = ("region_0", "region_1", "region_2")
REGION_BAND = ("region_0", "region_1", "region_2", "band")


def nothing_yet(x, identity):
    return jax.tree.map(
        lambda a, e: jnp.broadcast_to(jnp.asarray(e, a.dtype), a.shape), x, identity
    )


def all_in_one(x, axis):
    leaves = jax.tree.leaves(x)
    order = sorted(range(len(leaves)), key=lambda k: -leaves[k].size)
    width = (1, *leaves[order[0]].shape)[-1]
    lines = [
        jnp.pad(leaves[k].reshape(-1), (0, -leaves[k].size % width)).reshape(-1, width)
        for k in order
    ]
    both, at, found = (lax.all_gather(jnp.concatenate(lines), axis), 0, {})
    for k, line in zip(order, lines):
        slab = both[:, at : at + len(line)].reshape(len(both), -1)
        found[k] = slab[:, : leaves[k].size].reshape(-1, *leaves[k].shape)
        at += len(line)
    numbers = iter(range(len(leaves)))
    return jax.tree.map(lambda _: found[next(numbers)], x)


def prefix_by_axis(x, axes, combine, identity):
    before = start = nothing_yet(x, identity)
    running = x
    for axis in reversed(axes):
        size, index = (lax.axis_size(axis), lax.axis_index(axis))
        pieces = all_in_one(running, axis)
        inside, running = (start, start)
        for k in range(size):
            passed = k < index
            running = combine(running, jax.tree.map(lambda part: part[k], pieces))
            inside = jax.tree.map(lambda new, old: jnp.where(passed, new, old), running, inside)
        before = combine(inside, before)
    return before


def from_everyone(x, axis):
    size = lax.axis_size(axis)
    return lax.all_to_all(jnp.broadcast_to(x[None], (size, *x.shape)), axis, 0, 0, tiled=True)


def of_everyone(x, axis):
    everything = from_everyone(x, axis)
    return jnp.sum(everything, axis=0)


def over_axes(x, axes):
    far, near = axes
    return of_everyone(of_everyone(x, near), far)


def affine_link(earlier, trailing):
    return (earlier[0] * trailing[0], trailing[0] * earlier[1] + trailing[1])


def local(anomalies, operator, local_tile_index, err_std, err_corr):
    members = anomalies.shape[1]
    tile_width = operator.shape[2]
    blocks = operator.shape[0]
    band_size = lax.axis_size("band")
    devices = lax.axis_size(REGION) * lax.axis_size("band")
    tiles_here = anomalies.reshape(-1, tile_width, members)
    position = lax.axis_index("band")
    offsets = (jnp.arange(band_size, dtype=jnp.int32) - position) % band_size
    wanted = jnp.take(local_tile_index, offsets, axis=1).T
    asked_tiles = lax.all_to_all(wanted, "band", split_axis=0, concat_axis=0, tiled=True)
    served = jnp.take(tiles_here, asked_tiles.reshape(-1), axis=0)
    served = served.reshape(band_size, blocks, tile_width, members)
    arrived = lax.all_to_all(served, "band", split_axis=0, concat_axis=0, tiled=True)
    ops_seen = jnp.take(operator, offsets, axis=1)
    predicted = jnp.einsum("jdon,djnm->jom", ops_seen, arrived, preferred_element_type=jnp.float32)
    rescaled_values = predicted.reshape(-1, members) / err_std[:, None]
    decay_coef = err_corr[:, None]
    local_a, local_b = lax.associative_scan(affine_link, (decay_coef, rescaled_values), axis=0)
    identity_pair = (jnp.ones((1,), jnp.float32), jnp.zeros((members,), jnp.float32))
    carried = prefix_by_axis((local_a[-1], local_b[-1]), REGION_BAND, affine_link, identity_pair)
    whitened = local_b + local_a * carried[1][None, :]
    own_gram = lax.dot_general(
        whitened,
        whitened,
        (((0,), (0,)), ((), ())),
        precision=lax.Precision.HIGHEST,
        preferred_element_type=jnp.float32,
    )
    own_gram = own_gram + (members - 1.0) / devices * jnp.eye(members, dtype=jnp.float32)
    lower_factor = jnp.linalg.cholesky(
        over_axes(own_gram, (("region_0", "region_1"), ("region_2", "band")))
    )
    inverse = lax.linalg.triangular_solve(
        lower_factor,
        jnp.eye(members, dtype=jnp.float32),
        left_side=True,
        lower=True,
        transpose_a=True,
    )
    transform = (math.sqrt(members - 1.0) * inverse).astype(jnp.bfloat16)
    updated = jnp.dot(anomalies, transform, preferred_element_type=jnp.float32).astype(jnp.bfloat16)
    return (whitened, updated)


def solution(mesh):
    torus = Mesh(
        mesh.devices.reshape(4, 4, 2, mesh.shape["band"]),
        ("region_0", "region_1", "region_2", "band"),
    )
    placed = (
        P(REGION_BAND, None),
        P(REGION_BAND, None, None, None),
        P(REGION_BAND, None),
        P(REGION_BAND),
        P(REGION_BAND),
    )
    return jax.shard_map(
        local,
        mesh=torus,
        in_specs=placed,
        out_specs=(P(REGION_BAND, None), P(REGION_BAND, None)),
        check_vma=False,
    )
```

profile of v0, /device:TPU:1, one launch (start us, length us, event | category | flops | bytes accessed | tf_op | source)
XLA Modules:
  0.0 219.1 jit_solution(2414551837324282107)
XLA Ops:
  0.7 1.4 gather_fusion.1
  2.7 5.9 %all-to-all-start = ((s32[4,1,16]{2,1,0:T(1,128)}), s32[4,1,16]{2,1,0:T(1,128)S(1)}, u32[]{:S(2)}, u32[]{:S(2)}) async-start(s32[4,1,16]{2,1,0:T(1,128)} %bitcast.3), calls=%async_computation | async-start | bytes 4096 | tf_op jit(solution)/shard_map/all_to_all | solution.py:80
  21.3 4.3 %gather_fusion.2 = bf16[64,128,128]{2,1,0:T(8,128)(2,1)} fusion(bf16[128,128,128]{2,1,0:T(8,128)(2,1)} %bitcast.135, s32[1024]{0:T(1024)S(1)} %pad_clamp_fusion), kind=kCustom, calls=%fused_computation.2 | custom fusion | bytes 4194560 | tf_op jit(solution)/shard_map/jit(_take)/gather | solution.py:81
  25.6 3.2 %broadcast_select_fusion = bf16[4,16,128,128]{3,2,1,0:T(8,128)(2,1)} fusion(bf16[4,16,128,128]{3,2,1,0:T(8,128)(2,1)} %bitcast.136, pred[4,16]{1,0:T(4,128)(4,1)S(1)} %compare_and_fusion), kind=kLoop, calls=%fused_computation.9 | loop fusion | flops 1048576 | bytes 4194368 | tf_op jit(solution)/shard_map/jit(_take)/select_n | solution.py:81
  28.8 4.6 %all-to-all-start.1 = ((bf16[4,16,128,128]{3,2,1,0:T(8,128)(2,1)}), bf16[4,16,128,128]{3,2,1,0:T(8,128)(2,1)}, u32[]{:S(2)}, u32[]{:S(2)}) async-start(bf16[4,16,128,128]{3,2,1,0:T(8,128)(2,1)} %broadcast_select_fusion), calls=%async_computation.1 | async-start | bytes 4194304 | tf_op jit(solution)/shard_map/all_to_all | solution.py:83
  42.6 2.1 gather_fusion
  45.4 13.1 %all-to-all-done.1 = bf16[4,16,128,128]{3,2,1,0:T(8,128)(2,1)} async-done(((bf16[4,16,128,128]{3,2,1,0:T(8,128)(2,1)}), bf16[4,16,128,128]{3,2,1,0:T(8,128)(2,1)}, u32[]{:S(2)}, u32[]{:S(2)}) %all-to-all-start.1) | async-done | bytes 2097184 | tf_op jit(solution)/shard_map/all_to_all | solution.py:83
  58.5 3.0 %fusion.1 = f32[16,128,128,1]{2,1,0,3:T(8,128)S(1)} fusion(bf16[4,16,128,128]{3,2,1,0:T(8,128)(2,1)} %all-to-all-done.1, bf16[4,16,128,128]{3,2,1,0:T(8,128)(2,1)} %gather_fusion, pred[4]{0:T(512)(128)(4,1)S(1)} %compare_and_fusion.1), kind=kOutput, calls=%fused_computation.5 | convolution fusion | flops 269484032 | bytes 5242884 | tf_op jit(solution)/shard_map/jdon,djnm->jom/dot_general | solution.py:85
  61.8 2.2 %slice.567 = f32[1023,128]{1,0:T(8,128)} slice(f32[2048,128]{1,0:T(8,128)S(1)} %bitcast_divide_fusion), slice={[2:2048:2], [0:128:1]} | slice | bytes 1047552 | tf_op jit(solution)/shard_map/slice | solution.py:88
  64.0 2.1 slice.489
  66.1 2.0 slice.488
  68.1 1.4 multiply_add_fusion.1
  70.4 1.9 slice.565
  72.3 1.9 slice.495
  74.2 1.9 slice.494
  83.6 2.1 pad.167
  85.7 4.6 %pad.168 = f32[2048,128]{1,0:T(8,128)} pad(f32[1024,128]{1,0:T(8,128)} %add.538, f32[]{:T(128)} %constant.122.clone.1), padding=1_0_1x0_0_0 | pad | bytes 1572868 | tf_op jit(solution)/shard_map/pad | solution.py:88
  91.0 6.1 %all-gather.4 = f32[4,2,128]{2,1,0:T(2,128)S(1)} all-gather(f32[1,2,128]{2,1,0:T(2,128)S(1)} %maximum_bitcast_fusion), channel_id=2, replica_groups=mesh['region_0'=4,'region_1'=4,'region_2'=2,'band'=4] {'band'}, dimensions={0}, use_global_device_ids=true | all-gather | bytes 5120 | tf_op jit(solution)/shard_map/all_gather | solution.py:27
  100.9 1.9 fusion.39
  102.9 5.7 %all-gather.5 = f32[2,2,128]{2,1,0:T(2,128)S(1)} all-gather(f32[1,2,128]{2,1,0:T(2,128)S(1)} %maximum_bitcast_fusion.1), channel_id=3, replica_groups=mesh['region_0'=4,'region_1'=4,'region_2'=2,'band'=4] {'region_2'}, dimensions={0}, use_global_device_ids=true | all-gather | bytes 3072 | tf_op jit(solution)/shard_map/all_gather | solution.py:27
  113.0 7.7 %all-gather.6 = f32[4,2,128]{2,1,0:T(2,128)S(1)} all-gather(f32[1,2,128]{2,1,0:T(2,128)S(1)} %maximum_bitcast_fusion.2), channel_id=4, replica_groups=mesh['region_0'=4,'region_1'=4,'region_2'=2,'band'=4] {'region_1'}, dimensions={0}, use_global_device_ids=true | all-gather | bytes 5120 | tf_op jit(solution)/shard_map/all_gather | solution.py:27
  125.3 1.9 fusion.37
  127.2 8.1 %all-gather.7 = f32[4,2,128]{2,1,0:T(2,128)S(1)} all-gather(f32[1,2,128]{2,1,0:T(2,128)S(1)} %maximum_bitcast_fusion.3), channel_id=5, replica_groups=mesh['region_0'=4,'region_1'=4,'region_2'=2,'band'=4] {'region_0'}, dimensions={0}, use_global_device_ids=true | all-gather | bytes 5120 | tf_op jit(solution)/shard_map/all_gather | solution.py:27
  136.6 6.4 %add_bitcast_fusion = f32[128]{0:T(128)S(1)} fusion(pred[]{:T(512)S(6)} %gt.55, pred[]{:T(512)S(6)} %gt.54, pred[]{:T(512)S(6)} %gt.53, f32[4,2,128]{2,1,0:T(2,128)S(1)} %all-gather.7, pred[]{:T(512)S(6)} %gt.52, pred[]{:T(512)} %gt.51, pred[]{:T(512)} %gt.50, pred[]{:T(512)} %gt.49, pred[]{:T(512)} %gt.48, pred[]{:T(512)} %gt.47, pred[]{:T(512)} %gt.46, ...), kind=kLoop, calls=%fused_computation.131 | loop fusion | flops 5632 | bytes 7762 | tf_op jit(solution)/shard_map/add | solution.py:67
  143.1 1.9 multiply_add_fusion
  144.9 1.8 convolution_add_fusion
  146.8 16.8 %all_to_all.24 = f32[8,128,128]{2,1,0:T(8,128)} all-to-all(f32[8,128,128]{2,1,0:T(8,128)S(1)} %broadcast_in_dim.69), channel_id=1, replica_groups=mesh['region_0'=4,'region_1'=4,'region_2'=2,'band'=4] {'region_2','band'}, dimensions={0} | all-to-all | bytes 1048576 | tf_op jit(solution)/shard_map/all_to_all | solution.py:53
  164.8 19.3 %all_to_all.25 = f32[16,128,128]{2,1,0:T(8,128)S(1)} all-to-all(f32[16,128,128]{2,1,0:T(8,128)S(1)} %broadcast_in_dim.70), channel_id=1, replica_groups=mesh['region_0'=4,'region_1'=4,'region_2'=2,'band'=4] {'region_0','regio..., dimensions={0} | all-to-all | bytes 2097152 | tf_op jit(solution)/shard_map/all_to_all | solution.py:53
  184.3 11.7 %cholesky.17 = f32[128,128]{1,0:T(8,128)S(1)} custom-call(f32[128,128]{1,0:T(8,128)S(1)} %fusion.13), custom_call_target="Cholesky" | custom-call | tf_op jit(solution)/shard_map/jit(cholesky)/cholesky | solution.py:100
  197.3 9.8 %custom-call.6 = f32[1,128,128]{1,2,0:T(8,128)S(1)} custom-call(f32[1,128,128]{2,1,0:T(8,128)S(1)} %fusion.10), custom_call_target="InvertDiagBlocksLowerTriangular" | custom-call | tf_op jit(solution)/shard_map/triangular_solve | solution.py:103
  207.3 5.4 %fusion = bf16[16384,128]{0,1:T(8,128)(2,1)} fusion(bf16[128,128]{1,0:T(8,128)(2,1)S(1)} %fusion.5, bf16[16384,128]{1,0:T(8,128)(2,1)} %param.5), kind=kOutput, calls=%fused_computation.4 | convolution fusion | flops 538968064 | bytes 8421376 | tf_op jit(solution)/shard_map/dot_general | solution.py:111
  212.7 6.4 %copy.42 = bf16[16384,128]{1,0:T(8,128)(2,1)} copy(bf16[16384,128]{0,1:T(8,128)(2,1)} %fusion) | data formatting | bytes 8388608
  (242 shorter events, 36.0 us)
Async XLA Ops:
  0.6 41.9 %copy-start = (bf16[16,4,128,128]{3,2,1,0:T(8,128)(2,1)S(1)}, bf16[16,4,128,128]{3,2,1,0:T(8,128)(2,1)}, u32[]{:S(2)}) copy-start(bf16[16,4,128,128]{3,2,1,0:T(8,128)(2,1)} %param.6) | copy-start | bytes 6291460
  2.7 17.2 %all-to-all-start = ((s32[4,1,16]{2,1,0:T(1,128)}), s32[4,1,16]{2,1,0:T(1,128)S(1)}, u32[]{:S(2)}, u32[]{:S(2)}) async-start(s32[4,1,16]{2,1,0:T(1,128)} %bitcast.3), calls=%async_computation | async-start | bytes 4096 | tf_op jit(solution)/shard_map/all_to_all | solution.py:80
  28.8 4.6 %copy-start.5 = (f32[2048]{0:T(1024)S(1)}, f32[2048]{0:T(1024)}, u32[]{:S(2)}) copy-start(f32[2048]{0:T(1024)} %param.9) | copy-start | bytes 24580
  28.8 29.7 %all-to-all-start.1 = ((bf16[4,16,128,128]{3,2,1,0:T(8,128)(2,1)}), bf16[4,16,128,128]{3,2,1,0:T(8,128)(2,1)}, u32[]{:S(2)}, u32[]{:S(2)}) async-start(bf16[4,16,128,128]{3,2,1,0:T(8,128)(2,1)} %broadcast_select_fusion), calls=%async_computation.1 | async-start | bytes 4194304 | tf_op jit(solution)/shard_map/all_to_all | solution.py:83
  45.4 16.1 %copy-start.6 = (f32[2048]{0:T(1024)S(1)}, f32[2048]{0:T(1024)}, u32[]{:S(2)}) copy-start(f32[2048]{0:T(1024)} %param.8) | copy-start | bytes 24580
  61.8 7.7 %copy-start.2 = (f32[2048,128]{1,0:T(8,128)}, f32[2048,128]{1,0:T(8,128)S(1)}, u32[]{:S(2)}) copy-start(f32[2048,128]{1,0:T(8,128)S(1)} %bitcast_divide_fusion) | copy-start | bytes 3145732
  69.6 0.8 copy-start.4
  79.8 0.7 slice-start.1
  80.6 2.2 %slice-start = ((f32[2048,128]{1,0:T(8,128)}), f32[1,128]{1,0:T(1,128)S(1)}, s32[]{:S(2)}) async-start(f32[2048,128]{1,0:T(8,128)} %copy-done.2), calls=%async_computation.4 | async-start | bytes 1024 | tf_op jit(solution)/shard_map/slice | solution.py:88
  85.7 57.4 %copy-start.3 = (f32[2048,128]{1,0:T(8,128)}, f32[2048,128]{1,0:T(8,128)S(1)}, u32[]{:S(2)}) copy-start(f32[2048,128]{1,0:T(8,128)S(1)} %pad.167) | copy-start | bytes 3145732
  144.9 19.8 %copy-start.1 = (f32[2048,128]{1,0:T(8,128)}, f32[2048,128]{1,0:T(8,128)S(1)}, u32[]{:S(2)}) copy-start(f32[2048,128]{1,0:T(8,128)S(1)} %multiply_add_fusion) | copy-start | bytes 3145732
where the time goes:
time: 221 us; the launch traced here: 219 us
  blocking collectives  63.8 us (29%)
  other arithmetic  54.7 us (25%)
  local copies, waits for them, and re-layouts  52.2 us (24%)
  between operations  14.5 us (7%)
  waiting for transfers between devices  13.1 us (6%)
  starting transfers between devices  10.4 us (5%)
  matrix products  10.4 us (5%)
    all_to_all x2, blocking collectives, from_everyone(): lax.all_to_all(jnp.broadcast_to(x[None], (size, *x.shape)), axis, 0, 0, t...  36.1 us
    all_gather x4, blocking collectives, all_in_one(): both, at, found = (lax.all_gather(jnp.concatenate(lines), axis), 0, {})  27.7 us
    slice x75, local copies, waits for them, and re-layouts, local(): lax.associative_scan(affine_link, (decay_coef, rescaled_values), axis=0)  22.6 us
    add x24, other arithmetic, affine_link(): return (earlier[0] * trailing[0], trailing[0] * earlier[1] + trailing[1])  15.6 us
    all_to_all x1, waiting for transfers between devices, local(): lax.all_to_all(served, 'band', split_axis=0, concat_axis=0, tiled=True)  13.1 us
    another operation x3, other arithmetic, local(): jnp.linalg.cholesky(over_axes(own_gram, (('region_0', 'region_1'), ('regi...  12.4 us
    another operation x2, other arithmetic, local(): lax.linalg.triangular_solve(lower_factor, jnp.eye(members, dtype=jnp.floa...  10.5 us
    pad x40, local copies, waits for them, and re-layouts, local(): lax.associative_scan(affine_link, (decay_coef, rescaled_values), axis=0)  10.2 us
  transfers between devices with their start and end apart: 2, of which 1 were waited for; matrix products, arithmetic and copies ran while one was open for 10% of the time, Pallas kernels for 0%

commit v1 on v0

v1 whole, which is shorter than its diff:
```python
import functools
import math

import jax
import jax.numpy as jnp
from jax import lax
from jax.experimental import pallas as pl
from jax.experimental.pallas import tpu as pltpu
from jax.sharding import PartitionSpec as P

MESH = pl.DeviceIdType.MESH
HIGHEST = lax.Precision.HIGHEST
F32 = jnp.float32
BF16 = jnp.bfloat16

M = 128
BLK = 16
BAND = 4
CHUNK = 2
CHUNKS = BLK // CHUNK
NEAR = 8
FAR = 16
ROWS = M // NEAR


def block_scan(decay, value):
    row = lax.broadcasted_iota(jnp.int32, (M, M), 0)
    for d in (1, 2, 4):
        seen = row >= d
        before_v = jnp.where(seen, pltpu.roll(value, d, 0), 0.0)
        before_d = jnp.where(seen, pltpu.roll(decay, d, 0), 1.0)
        value = value + decay * before_v
        decay = decay * before_d
    for d in (8, 16, 32, 64):
        value = jnp.concatenate([value[:d], value[d:] + decay[d:] * value[:-d]], axis=0)
        decay = jnp.concatenate([decay[:d], decay[d:] * decay[:-d]], axis=0)
    return decay, value


def as_columns(row):
    return jnp.broadcast_to(row, (M, M)).T


def combine(n, me, rows_at, parts, left, right, whole):
    carry = jnp.zeros((1, M), F32)
    product = jnp.ones((1, M), F32)
    cross = jnp.zeros((1, M), F32)
    square = jnp.zeros((1, M), F32)
    own_carry, own_product = carry, product
    rows = jnp.zeros((ROWS, M), F32)
    for i in range(n):
        rows = rows + parts[i, 0:ROWS]
        state = parts[i, ROWS : ROWS + 8]
        a, b, h, s = (state[k : k + 1] for k in range(4))
        mine = me == i
        own_carry = jnp.where(mine, carry, own_carry)
        own_product = jnp.where(mine, product, own_product)
        u = h + s * carry
        left[i : i + 1, :] = h
        left[n + i : n + i + 1, :] = carry
        right[i : i + 1, :] = carry
        right[n + i : n + i + 1, :] = u
        cross = cross + product * u
        square = square + product * product * s
        carry = b + a * carry
        product = product * a
    whole[...] = jnp.dot(left[...].T, right[...], precision=HIGHEST, preferred_element_type=F32)
    rows = rows + whole[pl.ds(pl.multiple_of(rows_at, ROWS), ROWS), :]
    state = jnp.concatenate([product, carry, cross, square, jnp.zeros((4, M), F32)], axis=0)
    return rows, state, own_carry, own_product


def observe(
    anom_hbm, op_hbm, idx_vm, std_vm, corr_vm,
    gram_out, whit_out,
    anom, op, idx_own, idx_in, idx, send, recv, whit, prod, gram, msg1, in1, msg2, in2, l1, r1, l2, r2, whole, gram_in,
    load_sem, idx_sem, idx_send, idx_recv, tile_send, tile_recv, s1, q1, s2, q2, s3, q3,
):
    region, band = lax.axis_index("region"), lax.axis_index("band")
    column, core = region // 2, region % 2
    near = core * BAND + band

    load_anom = pltpu.make_async_copy(anom_hbm, anom, load_sem.at[0])
    load_op = pltpu.make_async_copy(op_hbm, op, load_sem.at[1])
    load_anom.start()
    load_op.start()

    def near_peer(e):
        p = (near + e) % NEAR
        return (column * 2 + p // BAND, p % BAND), p

    def far_peer(e):
        q = (column + e) % FAR
        return (q * 2 + core, band), q

    barrier = pltpu.get_barrier_semaphore()
    for e in range(1, NEAR):
        pl.semaphore_signal(barrier, inc=1, device_id=near_peer(e)[0], device_id_type=MESH)
    for e in range(1, FAR):
        pl.semaphore_signal(barrier, inc=1, device_id=far_peer(e)[0], device_id_type=MESH)

    idx_own[...] = jnp.zeros((8, M), jnp.int32)
    idx_own[0:BAND, 0:BLK] = idx_vm[...]
    own_idx = pltpu.make_async_copy(idx_own, idx.at[0], idx_sem.at[0])
    own_idx.start()
    pl.semaphore_wait(barrier, NEAR + FAR - 2)

    def idx_copy(e):
        return pltpu.make_async_remote_copy(
            src_ref=idx_own, dst_ref=idx_in.at[BAND - e], send_sem=idx_send.at[e], recv_sem=idx_recv.at[e],
            device_id=(region, (band + e) % BAND), device_id_type=MESH,
        )

    for e in (2, 1, 3):
        idx_copy(e).start()
    load_anom.wait()
    to_scalar = {}
    for e in (2, 1, 3):
        idx_copy(e).wait_recv()
        d = BAND - e
        to_scalar[d] = pltpu.make_async_copy(idx_in.at[d], idx.at[d], idx_sem.at[d])
        to_scalar[d].start()
    own_idx.wait()
    for e in (2, 1, 3):
        to_scalar[BAND - e].wait()

    def tile_copy(k, c):
        part = pl.ds(c * CHUNK, CHUNK)
        return pltpu.make_async_remote_copy(
            src_ref=send.at[k - 1, part], dst_ref=recv.at[k - 1, part],
            send_sem=tile_send.at[k - 1, c], recv_sem=tile_recv.at[k - 1, c],
            device_id=(region, (band + BAND - k) % BAND), device_id_type=MESH,
        )

    def serve(c, carry):
        for k in (2, 1, 3):
            for t in range(CHUNK):
                j = c * CHUNK + t
                send[k - 1, j] = anom[idx[BAND - k, k, j]]
            tile_copy(k, c).start()
        return carry

    lax.fori_loop(0, CHUNKS, serve, 0)
    load_op.wait()
    gram[...] = jnp.zeros((M, M), F32)

    def use(c, carry):
        last, product, cross, square = carry
        for k in (1, 3, 2):
            tile_copy(k, c).wait_recv()
        for t in range(CHUNK):
            j = c * CHUNK + t
            value = jnp.dot(op[j, 0], anom[idx[0, 0, j]], preferred_element_type=F32)
            for k in range(1, BAND):
                value = value + jnp.dot(op[j, k], recv[k - 1, j], preferred_element_type=F32)
            value = value * as_columns(1.0 / std_vm[pl.ds(j, 1), :])
            decay, value = block_scan(as_columns(corr_vm[pl.ds(j, 1), :]), value)
            value = value + decay * last
            decay = decay * product
            whit[j] = value
            prod[j] = decay
            last, product = value[M - 1 : M], decay[M - 1 : M]
            gram[...] += jnp.dot(value.T, value, precision=HIGHEST, preferred_element_type=F32)
            cross = cross + jnp.sum(value * decay, axis=0, keepdims=True)
            square = square + jnp.sum(decay * decay, axis=0, keepdims=True)
        return last, product, cross, square

    zero = jnp.zeros((1, M), F32)
    last, product, cross, square = lax.fori_loop(0, CHUNKS, use, (zero, jnp.ones((1, M), F32), zero, zero))

    state = jnp.concatenate([product, last, cross, square, jnp.zeros((4, M), F32)], axis=0)
    for p in range(NEAR):
        msg1[p, 0:ROWS] = gram[p * ROWS : (p + 1) * ROWS]
        msg1[p, ROWS : ROWS + 8] = state

    def copy1(e):
        device, p = near_peer(e)
        return pltpu.make_async_remote_copy(
            src_ref=msg1.at[p], dst_ref=in1.at[near], send_sem=s1.at[e], recv_sem=q1.at[e],
            device_id=device, device_id_type=MESH,
        )

    for e in range(1, NEAR):
        copy1(e).start()
    in1[near] = msg1[near]
    for e in range(1, NEAR):
        copy1(e).wait_recv()
    rows, state, own_carry, own_product = combine(NEAR, near, near * ROWS, in1, l1, r1, whole)
    msg2[0:ROWS] = rows
    msg2[ROWS : ROWS + 8] = state

    def copy2(e):
        device, _ = far_peer(e)
        return pltpu.make_async_remote_copy(
            src_ref=msg2, dst_ref=in2.at[column], send_sem=s2.at[e], recv_sem=q2.at[e],
            device_id=device, device_id_type=MESH,
        )

    for e in range(1, FAR):
        copy2(e).start()
    in2[column] = msg2[...]
    for e in range(1, FAR):
        copy2(e).wait_recv()
    rows, state, far_carry, _ = combine(FAR, column, near * ROWS, in2, l2, r2, whole)
    here = lax.broadcasted_iota(jnp.int32, (ROWS, M), 0) + near * ROWS
    lane = lax.broadcasted_iota(jnp.int32, (ROWS, M), 1)
    rows = rows + jnp.where(here == lane, M - 1.0, 0.0)
    own_rows = pl.ds(pl.multiple_of(near * ROWS, ROWS), ROWS)
    gram_in[own_rows, :] = rows

    def copy3(e):
        device, _ = near_peer(e)
        return pltpu.make_async_remote_copy(
            src_ref=gram_in.at[own_rows], dst_ref=gram_in.at[own_rows], send_sem=s3.at[e], recv_sem=q3.at[e],
            device_id=device, device_id_type=MESH,
        )

    for e in range(1, NEAR):
        copy3(e).start()

    before = own_carry + own_product * far_carry

    def settle(j, carry):
        whit[j] = whit[j] + prod[j] * before
        return carry

    lax.fori_loop(0, BLK, settle, 0)
    store = pltpu.make_async_copy(whit, whit_out, load_sem.at[0])
    store.start()
    for e in range(1, NEAR):
        copy3(e).wait_recv()
    gram_out[...] = gram_in[...]

    store.wait()
    for e in (2, 1, 3):
        idx_copy(e).wait_send()

    def drain(c, carry):
        for k in range(1, BAND):
            tile_copy(k, c).wait_send()
        return carry

    lax.fori_loop(0, CHUNKS, drain, 0)
    for e in range(1, NEAR):
        copy1(e).wait_send()
        copy3(e).wait_send()
    for e in range(1, FAR):
        copy2(e).wait_send()


def inverse_factor(work, gram):
    n = M // 8
    lane = lax.broadcasted_iota(jnp.int32, (8, M), 1)
    sub = lax.broadcasted_iota(jnp.int32, (8, M), 0)
    rows = [gram[8 * i : 8 * i + 8, :] for i in range(n)]
    done = []
    for p in range(n):
        base = 8 * p
        block = rows[p]
        cols = [jnp.broadcast_to(block[:, base + l : base + l + 1], (8, M)) for l in range(8)]
        s = [[jnp.broadcast_to(cols[l][j : j + 1, :], (8, M)) for l in range(8)] for j in range(8)]
        inside = (lane >= base) & (lane < base + 8)
        r = []
        for j in range(8):
            own = jnp.broadcast_to(block[j : j + 1, :], (8, M))
            r.append(jnp.where(inside, jnp.where(lane == base + j, 1.0, 0.0), own))
        lower, pivot = [], []
        for j in range(8):
            inv = 1.0 / s[j][j]
            lower.append(r[j])
            pivot.append(s[j][j])
            for i in range(8):
                if i == j:
                    continue
                f = s[i][j] * inv
                for l in range(j + 1, 8):
                    s[i][l] = s[i][l] - f * s[j][l]
                r[i] = r[i] - f * r[j]
            for l in range(j + 1, 8):
                s[j][l] = s[j][l] * inv
            r[j] = r[j] * inv
            s[j][j] = None
        out = lower[0]
        d = pivot[0]
        for j in range(1, 8):
            out = jnp.where(sub == j, lower[j], out)
            d = jnp.where(sub == j, pivot[j], d)
        keep = lane <= base + sub
        done.append(jnp.where(keep, out * lax.rsqrt(d), 0.0))
        for i in range(p + 1, n):
            t = jnp.where(inside, 0.0, rows[i])
            for l in range(8):
                t = t - jnp.broadcast_to(rows[i][:, base + l : base + l + 1], (8, M)) * r[l]
            rows[i] = t
    for p in range(n):
        work[8 * p : 8 * p + 8, :] = done[p]


PIECES = 8
PIECE = 128 * M // PIECES


def analyse(gram, anom_hbm, out_hbm, anom, out, work, in_sem, out_sem):
    def load(i):
        at = pl.ds(i * PIECE, PIECE)
        return pltpu.make_async_copy(anom_hbm.at[at], anom.at[at], in_sem.at[i])

    def store(i):
        at = pl.ds(i * PIECE, PIECE)
        return pltpu.make_async_copy(out.at[at], out_hbm.at[at], out_sem.at[i])

    for i in range(PIECES):
        load(i).start()
    inverse_factor(work, gram[...])
    transform = (math.sqrt(M - 1.0) * work[...].T).astype(BF16)
    for i in range(PIECES):
        load(i).wait()
        at = pl.ds(i * PIECE, PIECE)
        out[at, :] = jnp.dot(anom[at, :], transform, preferred_element_type=F32).astype(BF16)
        store(i).start()
    for i in range(PIECES):
        store(i).wait()


def local(anomalies, operator, local_tile_index, err_std, err_corr):
    any_spec = pl.BlockSpec(memory_space=pl.ANY)
    vmem = pl.BlockSpec(memory_space=pltpu.VMEM)
    dma = pltpu.SemaphoreType.DMA
    gram, whitened = pl.pallas_call(
        observe,
        out_shape=(jax.ShapeDtypeStruct((M, M), F32), jax.ShapeDtypeStruct((BLK, M, M), F32)),
        in_specs=[any_spec, any_spec, vmem, vmem, vmem],
        out_specs=(vmem, any_spec),
        scratch_shapes=[
            pltpu.VMEM((M, M, M), BF16),
            pltpu.VMEM((BLK, BAND, M, M), BF16),
            pltpu.VMEM((8, M), jnp.int32),
            pltpu.VMEM((BAND, 8, M), jnp.int32),
            pltpu.SMEM((BAND, 8, M), jnp.int32),
            pltpu.VMEM((BAND - 1, BLK, M, M), BF16),
            pltpu.VMEM((BAND - 1, BLK, M, M), BF16),
            pltpu.VMEM((BLK, M, M), F32),
            pltpu.VMEM((BLK, M, M), F32),
            pltpu.VMEM((M, M), F32),
            pltpu.VMEM((NEAR, ROWS + 8, M), F32),
            pltpu.VMEM((NEAR, ROWS + 8, M), F32),
            pltpu.VMEM((ROWS + 8, M), F32),
            pltpu.VMEM((FAR, ROWS + 8, M), F32),
            pltpu.VMEM((2 * NEAR, M), F32),
            pltpu.VMEM((2 * NEAR, M), F32),
            pltpu.VMEM((2 * FAR, M), F32),
            pltpu.VMEM((2 * FAR, M), F32),
            pltpu.VMEM((M, M), F32),
            pltpu.VMEM((M, M), F32),
            dma((2,)),
            dma((BAND,)),
            dma((BAND,)),
            dma((BAND,)),
            dma((BAND - 1, CHUNKS)),
            dma((BAND - 1, CHUNKS)),
            dma((NEAR,)),
            dma((NEAR,)),
            dma((FAR,)),
            dma((FAR,)),
            dma((NEAR,)),
            dma((NEAR,)),
        ],
        compiler_params=pltpu.CompilerParams(
            collective_id=0, has_side_effects=True, vmem_limit_bytes=32 * 1024 * 1024
        ),
        name="observe",
    )(
        anomalies.reshape(M, M, M),
        operator,
        local_tile_index.T,
        err_std.reshape(BLK, M),
        err_corr.reshape(BLK, M),
    )
    updated = pl.pallas_call(
        analyse,
        out_shape=jax.ShapeDtypeStruct((M * M, M), BF16),
        in_specs=[vmem, any_spec],
        out_specs=any_spec,
        scratch_shapes=[
            pltpu.VMEM((M * M, M), BF16),
            pltpu.VMEM((M * M, M), BF16),
            pltpu.VMEM((M, M), F32),
            dma((PIECES,)),
            dma((PIECES,)),
        ],
        compiler_params=pltpu.CompilerParams(vmem_limit_bytes=32 * 1024 * 1024),
        name="analyse",
    )(gram, anomalies)
    return whitened.reshape(BLK * M, M), updated


def solution(mesh):
    both = ("region", "band")
    return jax.shard_map(
        local,
        mesh=mesh,
        in_specs=(P(both, None), P(both, None, None, None), P(both, None), P(both), P(both)),
        out_specs=(P(both, None), P(both, None)),
        check_vma=False,
    )
```

time: 221 us -> 68.6 us (0.31)
  blocking collectives: 63.8 us -> 0 us
  Pallas kernels: 0 us -> 60.8 us
  other arithmetic: 54.7 us -> 0 us
  local copies, waits for them, and re-layouts: 52.2 us -> 6.82 us
  between operations: 14.5 us -> 0.66 us
  waiting for transfers between devices: 13.1 us -> 0 us
  matrix products: 10.4 us -> 0 us
  starting transfers between devices: 10.4 us -> 0 us
    pallas_call x0 -> x2, Pallas kernels: none -> 60.8 us  [the longest x1 51.8 us: local(): pl.pallas_call(observe, out_shape=(jax.ShapeDtypeStruct((M, M), F32), jax...]
    all_to_all x2 -> x0, blocking collectives: 36.1 us -> none  [from_everyone(): lax.all_to_all(jnp.broadcast_to(x[None], (size, *x.shape)), axis, 0, 0, t...]
    all_gather x4 -> x0, blocking collectives: 27.7 us -> none  [all_in_one(): both, at, found = (lax.all_gather(jnp.concatenate(lines), axis), 0, {})]
    slice x84 -> x0, local copies, waits for them, and re-layouts: 25.5 us -> none  [the longest x75 22.6 us: local(): lax.associative_scan(affine_link, (decay_coef, rescaled_values), axis=0)]
    another operation x5 -> x0, other arithmetic: 22.9 us -> none  [the longest x3 12.4 us: local(): jnp.linalg.cholesky(over_axes(own_gram, (('region_0', 'region_1'), ('regi...]
    add x47 -> x0, other arithmetic: 19.9 us -> none  [the longest x24 15.6 us: affine_link(): return (earlier[0] * trailing[0], trailing[0] * earlier[1] + trailing[1])]
    all_to_all x2 -> x0, waiting for transfers between devices: 13.1 us -> none  [the longest x1 13.1 us: local(): lax.all_to_all(served, 'band', split_axis=0, concat_axis=0, tiled=True)]
    all_to_all x2 -> x0, starting transfers between devices: 10.4 us -> none  [the longest x1 5.86 us: local(): lax.all_to_all(wanted, 'band', split_axis=0, concat_axis=0, tiled=True)]
  transfers between devices with their start and end apart: 2 -> 0, of which waited for: 1 -> 0; matrix products, arithmetic and copies ran while one was open for 10% -> 0% of each run, Pallas kernels for 0% -> 0%
where the time goes in v1:
time: 68.6 us; the launch traced here: 68.3 us
  Pallas kernels  60.8 us (89%)
  local copies, waits for them, and re-layouts  6.82 us (10%)
    pallas_call x1, Pallas kernels, local(): pl.pallas_call(observe, out_shape=(jax.ShapeDtypeStruct((M, M), F32), jax...  51.8 us
    pallas_call x1, Pallas kernels, local(): pl.pallas_call(analyse, out_shape=jax.ShapeDtypeStruct((M * M, M), BF16),...  8.99 us
    unnamed x11, local copies, waits for them, and re-layouts  6.82 us

profile of v1, /device:TPU:1, one launch (start us, length us, event | category | flops | bytes accessed | tf_op | source)
XLA Modules:
  0.0 68.3 jit_solution(16329180461836606835)
XLA Ops:
  0.6 0.0 copy-start
  0.6 2.2 %copy-done = bf16[16384,128]{1,0:T(8,128)(2,1)S(1)} copy-done((bf16[16384,128]{1,0:T(8,128)(2,1)S(1)}, bf16[16384,128]{1,0:T(8,128)(2,1)}, u32[]{:S(2)}) %copy-start) | copy-done | bytes 4194328
  2.8 0.0 copy-start.1
  2.8 1.6 %copy-done.1 = bf16[16,4,128,128]{3,2,1,0:T(8,128)(2,1)S(1)} copy-done((bf16[16,4,128,128]{3,2,1,0:T(8,128)(2,1)S(1)}, bf16[16,4,128,128]{3,2,1,0:T(8,128)(2,1)}, u32[]{:S(2)}) %copy-start.1) | copy-done | bytes 2097176
  4.4 0.0 copy-start.2
  4.4 0.7 %copy-done.2 = f32[2048]{0:T(1024)S(1)} copy-done((f32[2048]{0:T(1024)S(1)}, f32[2048]{0:T(1024)}, u32[]{:S(2)}) %copy-start.2) | copy-done | bytes 8216
  5.1 0.0 copy-start.3
  5.1 0.7 %copy-done.3 = f32[2048]{0:T(1024)S(1)} copy-done((f32[2048]{0:T(1024)S(1)}, f32[2048]{0:T(1024)}, u32[]{:S(2)}) %copy-start.3) | copy-done | bytes 8216
  5.8 0.0 copy-start.4
  5.8 0.7 copy-done.4
  6.5 51.8 %observe.1 = (f32[128,128]{1,0:T(8,128)S(1)}, f32[16,128,128]{2,1,0:T(8,128)S(1)}) custom-call(bf16[128,128,128]{2,1,0:T(8,128)(2,1)S(1)} %bitcast.5, bf16[16,4,128,128]{3,2,1,0:T(8,128)(2,1)S(1)} %copy-done.1, s32[4,16]{1,0:T(4,128)S(1)} %bitcast.9, f32[16,128]{1,0:T(8,128)S(1)} %bitcast.7, f32[16,128]{1,0:T(8,128)S(1)} %bitcast.8), custom_call_target="tpu_custom_call" | custom-call | tf_op jit(solution)/shard_map/observe/pallas_call | solution.py:329
  58.3 9.0 %analyse.1 = bf16[16384,128]{1,0:T(8,128)(2,1)} custom-call(f32[128,128]{1,0:T(8,128)S(1)} %get-tuple-element.5.gram, bf16[16384,128]{1,0:T(8,128)(2,1)S(1)} %copy-done), custom_call_target="tpu_custom_call" | custom-call | tf_op jit(solution)/shard_map/analyse/pallas_call | solution.py:379
  67.3 1.0 %copy.8 = f32[2048,128]{1,0:T(8,128)} copy(f32[2048,128]{1,0:T(8,128)S(1)} %bitcast.6) | data formatting | bytes 2097152
Async XLA Ops:
  0.6 2.2 %copy-start = (bf16[16384,128]{1,0:T(8,128)(2,1)S(1)}, bf16[16384,128]{1,0:T(8,128)(2,1)}, u32[]{:S(2)}) copy-start(bf16[16384,128]{1,0:T(8,128)(2,1)} %anom_hbm.1) | copy-start | bytes 12582916
  2.8 1.6 %copy-start.1 = (bf16[16,4,128,128]{3,2,1,0:T(8,128)(2,1)S(1)}, bf16[16,4,128,128]{3,2,1,0:T(8,128)(2,1)}, u32[]{:S(2)}) copy-start(bf16[16,4,128,128]{3,2,1,0:T(8,128)(2,1)} %op_hbm.1) | copy-start | bytes 6291460
  4.4 0.7 %copy-start.2 = (f32[2048]{0:T(1024)S(1)}, f32[2048]{0:T(1024)}, u32[]{:S(2)}) copy-start(f32[2048]{0:T(1024)} %param.8) | copy-start | bytes 24580
  5.1 0.7 %copy-start.3 = (f32[2048]{0:T(1024)S(1)}, f32[2048]{0:T(1024)}, u32[]{:S(2)}) copy-start(f32[2048]{0:T(1024)} %param.9) | copy-start | bytes 24580
  5.8 0.7 copy-start.4

commit v2 on v1

--- a/solution.py
+++ b/solution.py
@@ -16,11 +16,13 @@
 M = 128
 BLK = 16
 BAND = 4
-CHUNK = 2
+CHUNK = 1
 CHUNKS = BLK // CHUNK
+HALF = CHUNKS // 2
 NEAR = 8
 FAR = 16
 ROWS = M // NEAR
+VMEM_BYTES = 60 * 1024 * 1024
 
 
 def block_scan(decay, value):
@@ -71,9 +73,9 @@
 
 
 def observe(
-    anom_hbm, op_hbm, idx_vm, std_vm, corr_vm,
+    anom_hbm, op_hbm, idx_hbm, std_hbm, corr_hbm,
     gram_out, whit_out,
-    anom, op, idx_own, idx_in, idx, send, recv, whit, prod, gram, msg1, in1, msg2, in2, l1, r1, l2, r2, whole, gram_in,
+    anom, op, idx_vm, std_vm, corr_vm, idx_own, idx_in, idx, send, recv, whit, prod, gram, msg1, in1, msg2, in2, l1, r1, l2, r2, whole, gram_in,
     load_sem, idx_sem, idx_send, idx_recv, tile_send, tile_recv, s1, q1, s2, q2, s3, q3,
 ):
     region, band = lax.axis_index("region"), lax.axis_index("band")
@@ -82,7 +84,13 @@
 
     load_anom = pltpu.make_async_copy(anom_hbm, anom, load_sem.at[0])
     load_op = pltpu.make_async_copy(op_hbm, op, load_sem.at[1])
+    load_idx = pltpu.make_async_copy(idx_hbm, idx_vm, load_sem.at[2])
+    load_std = pltpu.make_async_copy(std_hbm, std_vm, load_sem.at[3])
+    load_corr = pltpu.make_async_copy(corr_hbm, corr_vm, load_sem.at[4])
+    load_idx.start()
     load_anom.start()
+    load_std.start()
+    load_corr.start()
     load_op.start()
 
     def near_peer(e):
@@ -99,9 +107,10 @@
     for e in range(1, FAR):
         pl.semaphore_signal(barrier, inc=1, device_id=far_peer(e)[0], device_id_type=MESH)
 
+    load_idx.wait()
     idx_own[...] = jnp.zeros((8, M), jnp.int32)
     idx_own[0:BAND, 0:BLK] = idx_vm[...]
-    own_idx = pltpu.make_async_copy(idx_own, idx.at[0], idx_sem.at[0])
+    own_idx = pltpu.make_async_copy(idx_own, idx.at[0], load_sem.at[2])
     own_idx.start()
     pl.semaphore_wait(barrier, NEAR + FAR - 2)
 
@@ -111,18 +120,9 @@
             device_id=(region, (band + e) % BAND), device_id_type=MESH,
         )
 
-    for e in (2, 1, 3):
+    for e in (1, 3, 2):
         idx_copy(e).start()
     load_anom.wait()
-    to_scalar = {}
-    for e in (2, 1, 3):
-        idx_copy(e).wait_recv()
-        d = BAND - e
-        to_scalar[d] = pltpu.make_async_copy(idx_in.at[d], idx.at[d], idx_sem.at[d])
-        to_scalar[d].start()
-    own_idx.wait()
-    for e in (2, 1, 3):
-        to_scalar[BAND - e].wait()
 
     def tile_copy(k, c):
         part = pl.ds(c * CHUNK, CHUNK)
@@ -132,15 +132,39 @@
             device_id=(region, (band + BAND - k) % BAND), device_id_type=MESH,
         )
 
-    def serve(c, carry):
-        for k in (2, 1, 3):
-            for t in range(CHUNK):
-                j = c * CHUNK + t
-                send[k - 1, j] = anom[idx[BAND - k, k, j]]
-            tile_copy(k, c).start()
+    def serve(k, c):
+        for t in range(CHUNK):
+            j = c * CHUNK + t
+            send[k - 1, j] = anom[idx[BAND - k, k, j]]
+        tile_copy(k, c).start()
+
+    def serve_sides(c, carry):
+        serve(1, c)
+        serve(3, c)
         return carry
 
-    lax.fori_loop(0, CHUNKS, serve, 0)
+    def serve_all(c, carry):
+        serve(2, c)
+        serve(2, c + HALF)
+        serve_sides(c + HALF, 0)
+        return carry
+
+    def to_scalar(e):
+        return pltpu.make_async_copy(idx_in.at[BAND - e], idx.at[BAND - e], idx_sem.at[e])
+
+    for e in (1, 3):
+        idx_copy(e).wait_recv()
+        to_scalar(e).start()
+    for e in (1, 3):
+        to_scalar(e).wait()
+    lax.fori_loop(0, HALF, serve_sides, 0)
+    idx_copy(2).wait_recv()
+    to_scalar(2).start()
+    to_scalar(2).wait()
+    lax.fori_loop(0, HALF, serve_all, 0)
+    own_idx.wait()
+    load_std.wait()
+    load_corr.wait()
     load_op.wait()
     gram[...] = jnp.zeros((M, M), F32)
 
@@ -300,7 +324,7 @@
 PIECE = 128 * M // PIECES
 
 
-def analyse(gram, anom_hbm, out_hbm, anom, out, work, in_sem, out_sem):
+def analyse(gram, whit_hbm, anom_hbm, whit_out, out_hbm, anom, whit, out, work, in_sem, out_sem, whit_sem):
     def load(i):
         at = pl.ds(i * PIECE, PIECE)
         return pltpu.make_async_copy(anom_hbm.at[at], anom.at[at], in_sem.at[i])
@@ -309,8 +333,13 @@
         at = pl.ds(i * PIECE, PIECE)
         return pltpu.make_async_copy(out.at[at], out_hbm.at[at], out_sem.at[i])
 
+    load_whit = pltpu.make_async_copy(whit_hbm, whit, whit_sem.at[0])
+    store_whit = pltpu.make_async_copy(whit, whit_out, whit_sem.at[1])
+    load_whit.start()
     for i in range(PIECES):
         load(i).start()
+    load_whit.wait()
+    store_whit.start()
     inverse_factor(work, gram[...])
     transform = (math.sqrt(M - 1.0) * work[...].T).astype(BF16)
     for i in range(PIECES):
@@ -318,6 +347,7 @@
         at = pl.ds(i * PIECE, PIECE)
         out[at, :] = jnp.dot(anom[at, :], transform, preferred_element_type=F32).astype(BF16)
         store(i).start()
+    store_whit.wait()
     for i in range(PIECES):
         store(i).wait()
 
@@ -329,11 +359,14 @@
     gram, whitened = pl.pallas_call(
         observe,
         out_shape=(jax.ShapeDtypeStruct((M, M), F32), jax.ShapeDtypeStruct((BLK, M, M), F32)),
-        in_specs=[any_spec, any_spec, vmem, vmem, vmem],
+        in_specs=[any_spec] * 5,
         out_specs=(vmem, any_spec),
         scratch_shapes=[
             pltpu.VMEM((M, M, M), BF16),
             pltpu.VMEM((BLK, BAND, M, M), BF16),
+            pltpu.VMEM((BAND, BLK), jnp.int32),
+            pltpu.VMEM((BLK, M), F32),
+            pltpu.VMEM((BLK, M), F32),
             pltpu.VMEM((8, M), jnp.int32),
             pltpu.VMEM((BAND, 8, M), jnp.int32),
             pltpu.SMEM((BAND, 8, M), jnp.int32),
@@ -352,7 +385,7 @@
             pltpu.VMEM((2 * FAR, M), F32),
             pltpu.VMEM((M, M), F32),
             pltpu.VMEM((M, M), F32),
-            dma((2,)),
+            dma((5,)),
             dma((BAND,)),
             dma((BAND,)),
             dma((BAND,)),
@@ -366,7 +399,7 @@
             dma((NEAR,)),
         ],
         compiler_params=pltpu.CompilerParams(
-            collective_id=0, has_side_effects=True, vmem_limit_bytes=32 * 1024 * 1024
+            collective_id=0, has_side_effects=True, vmem_limit_bytes=VMEM_BYTES
         ),
         name="observe",
     )(
@@ -376,22 +409,24 @@
         err_std.reshape(BLK, M),
         err_corr.reshape(BLK, M),
     )
-    updated = pl.pallas_call(
+    whitened, updated = pl.pallas_call(
         analyse,
-        out_shape=jax.ShapeDtypeStruct((M * M, M), BF16),
-        in_specs=[vmem, any_spec],
-        out_specs=any_spec,
+        out_shape=(jax.ShapeDtypeStruct((BLK * M, M), F32), jax.ShapeDtypeStruct((M * M, M), BF16)),
+        in_specs=[vmem, any_spec, any_spec],
+        out_specs=(any_spec, any_spec),
         scratch_shapes=[
             pltpu.VMEM((M * M, M), BF16),
+            pltpu.VMEM((BLK * M, M), F32),
             pltpu.VMEM((M * M, M), BF16),
             pltpu.VMEM((M, M), F32),
             dma((PIECES,)),
             dma((PIECES,)),
+            dma((2,)),
         ],
-        compiler_params=pltpu.CompilerParams(vmem_limit_bytes=32 * 1024 * 1024),
+        compiler_params=pltpu.CompilerParams(vmem_limit_bytes=VMEM_BYTES),
         name="analyse",
-    )(gram, anomalies)
-    return whitened.reshape(BLK * M, M), updated
+    )(gram, whitened.reshape(BLK * M, M), anomalies)
+    return whitened, updated
 
 
 def solution(mesh):

time: 68.6 us -> 68.1 us (level)
  local copies, waits for them, and re-layouts: 6.82 us -> 0 us
  Pallas kernels: 60.8 us -> 67.3 us
    unnamed x11 -> x0, local copies, waits for them, and re-layouts: 6.82 us -> none
    pallas_call x1, Pallas kernels: 51.8 us -> 55.4 us  [local(): pl.pallas_call(observe, out_shape=(jax.ShapeDtypeStruct((M, M), F32), jax...]
    pallas_call x1, Pallas kernels: 8.99 us -> 11.9 us  [local(): pl.pallas_call(analyse, out_shape=(jax.ShapeDtypeStruct((BLK * M, M), F32...]
where the time goes in v2:
time: 68.1 us; the launch traced here: 67.9 us
  Pallas kernels  67.3 us (99%)
    pallas_call x1, Pallas kernels, local(): pl.pallas_call(observe, out_shape=(jax.ShapeDtypeStruct((M, M), F32), jax...  55.4 us
    pallas_call x1, Pallas kernels, local(): pl.pallas_call(analyse, out_shape=(jax.ShapeDtypeStruct((BLK * M, M), F32...  11.9 us

profile of v2, /device:TPU:1, one launch (start us, length us, event | category | flops | bytes accessed | tf_op | source)
XLA Modules:
  0.0 67.9 jit_solution(6757864325252669911)
XLA Ops:
  0.6 55.4 %observe.1 = (f32[128,128]{1,0:T(8,128)}, f32[16,128,128]{2,1,0:T(8,128)}) custom-call(bf16[128,128,128]{2,1,0:T(8,128)(2,1)} %bitcast.5, bf16[16,4,128,128]{3,2,1,0:T(8,128)(2,1)} %op_hbm.1, s32[4,16]{1,0:T(4,128)} %bitcast.9, f32[16,128]{1,0:T(8,128)} %bitcast.7, f32[16,128]{1,0:T(8,128)} %bitcast.8), custom_call_target="tpu_custom_call" | custom-call | tf_op jit(solution)/shard_map/observe/pallas_call | solution.py:359
  56.0 11.9 %analyse.1 = (f32[2048,128]{1,0:T(8,128)}, bf16[16384,128]{1,0:T(8,128)(2,1)}) custom-call(f32[128,128]{1,0:T(8,128)} %get-tuple-element.4.gram, f32[2048,128]{1,0:T(8,128)} %bitcast.6, bf16[16384,128]{1,0:T(8,128)(2,1)} %anom_hbm.1), custom_call_target="tpu_custom_call" | custom-call | tf_op jit(solution)/shard_map/analyse/pallas_call | solution.py:412

commit v3 on v2

--- a/solution.py
+++ b/solution.py
@@ -22,7 +22,8 @@
 NEAR = 8
 FAR = 16
 ROWS = M // NEAR
-VMEM_BYTES = 60 * 1024 * 1024
+OBSERVE_VMEM = 52 * 1024 * 1024
+ANALYSE_VMEM = 16 * 1024 * 1024
 
 
 def block_scan(decay, value):
@@ -74,8 +75,8 @@
 
 def observe(
     anom_hbm, op_hbm, idx_hbm, std_hbm, corr_hbm,
-    gram_out, whit_out,
-    anom, op, idx_vm, std_vm, corr_vm, idx_own, idx_in, idx, send, recv, whit, prod, gram, msg1, in1, msg2, in2, l1, r1, l2, r2, whole, gram_in,
+    gram_out, whit, anom,
+    op, idx_vm, std_vm, corr_vm, idx_own, idx_in, idx, send, recv, prod, gram, msg1, in1, msg2, in2, l1, r1, l2, r2, whole, gram_in,
     load_sem, idx_sem, idx_send, idx_recv, tile_send, tile_recv, s1, q1, s2, q2, s3, q3,
 ):
     region, band = lax.axis_index("region"), lax.axis_index("band")
@@ -249,13 +250,10 @@
         return carry
 
     lax.fori_loop(0, BLK, settle, 0)
-    store = pltpu.make_async_copy(whit, whit_out, load_sem.at[0])
-    store.start()
     for e in range(1, NEAR):
         copy3(e).wait_recv()
     gram_out[...] = gram_in[...]
 
-    store.wait()
     for e in (2, 1, 3):
         idx_copy(e).wait_send()
 
@@ -324,26 +322,16 @@
 PIECE = 128 * M // PIECES
 
 
-def analyse(gram, whit_hbm, anom_hbm, whit_out, out_hbm, anom, whit, out, work, in_sem, out_sem, whit_sem):
-    def load(i):
-        at = pl.ds(i * PIECE, PIECE)
-        return pltpu.make_async_copy(anom_hbm.at[at], anom.at[at], in_sem.at[i])
-
+def analyse(gram, whit, anom, whit_out, out_hbm, out, work, out_sem, whit_sem):
     def store(i):
         at = pl.ds(i * PIECE, PIECE)
         return pltpu.make_async_copy(out.at[at], out_hbm.at[at], out_sem.at[i])
 
-    load_whit = pltpu.make_async_copy(whit_hbm, whit, whit_sem.at[0])
-    store_whit = pltpu.make_async_copy(whit, whit_out, whit_sem.at[1])
-    load_whit.start()
-    for i in range(PIECES):
-        load(i).start()
-    load_whit.wait()
+    store_whit = pltpu.make_async_copy(whit, whit_out, whit_sem)
     store_whit.start()
     inverse_factor(work, gram[...])
     transform = (math.sqrt(M - 1.0) * work[...].T).astype(BF16)
     for i in range(PIECES):
-        load(i).wait()
         at = pl.ds(i * PIECE, PIECE)
         out[at, :] = jnp.dot(anom[at, :], transform, preferred_element_type=F32).astype(BF16)
         store(i).start()
@@ -356,13 +344,16 @@
     any_spec = pl.BlockSpec(memory_space=pl.ANY)
     vmem = pl.BlockSpec(memory_space=pltpu.VMEM)
     dma = pltpu.SemaphoreType.DMA
-    gram, whitened = pl.pallas_call(
+    gram, whitened, held = pl.pallas_call(
         observe,
-        out_shape=(jax.ShapeDtypeStruct((M, M), F32), jax.ShapeDtypeStruct((BLK, M, M), F32)),
+        out_shape=(
+            pltpu.VMEM((M, M), F32),
+            pltpu.VMEM((BLK, M, M), F32),
+            pltpu.VMEM((M, M, M), BF16),
+        ),
         in_specs=[any_spec] * 5,
-        out_specs=(vmem, any_spec),
+        out_specs=(vmem, vmem, vmem),
         scratch_shapes=[
-            pltpu.VMEM((M, M, M), BF16),
             pltpu.VMEM((BLK, BAND, M, M), BF16),
             pltpu.VMEM((BAND, BLK), jnp.int32),
             pltpu.VMEM((BLK, M), F32),
@@ -372,7 +363,6 @@
             pltpu.SMEM((BAND, 8, M), jnp.int32),
             pltpu.VMEM((BAND - 1, BLK, M, M), BF16),
             pltpu.VMEM((BAND - 1, BLK, M, M), BF16),
-            pltpu.VMEM((BLK, M, M), F32),
             pltpu.VMEM((BLK, M, M), F32),
             pltpu.VMEM((M, M), F32),
             pltpu.VMEM((NEAR, ROWS + 8, M), F32),
@@ -399,7 +389,7 @@
             dma((NEAR,)),
         ],
         compiler_params=pltpu.CompilerParams(
-            collective_id=0, has_side_effects=True, vmem_limit_bytes=VMEM_BYTES
+            collective_id=0, has_side_effects=True, vmem_limit_bytes=OBSERVE_VMEM
         ),
         name="observe",
     )(
@@ -412,20 +402,17 @@
     whitened, updated = pl.pallas_call(
         analyse,
         out_shape=(jax.ShapeDtypeStruct((BLK * M, M), F32), jax.ShapeDtypeStruct((M * M, M), BF16)),
-        in_specs=[vmem, any_spec, any_spec],
+        in_specs=[vmem, vmem, vmem],
         out_specs=(any_spec, any_spec),
         scratch_shapes=[
             pltpu.VMEM((M * M, M), BF16),
-            pltpu.VMEM((BLK * M, M), F32),
-            pltpu.VMEM((M * M, M), BF16),
             pltpu.VMEM((M, M), F32),
             dma((PIECES,)),
-            dma((PIECES,)),
-            dma((2,)),
+            dma,
         ],
-        compiler_params=pltpu.CompilerParams(vmem_limit_bytes=VMEM_BYTES),
+        compiler_params=pltpu.CompilerParams(vmem_limit_bytes=ANALYSE_VMEM),
         name="analyse",
-    )(gram, whitened.reshape(BLK * M, M), anomalies)
+    )(gram, whitened.reshape(BLK * M, M), held.reshape(M * M, M))
     return whitened, updated
 
 

time: 68.1 us -> 63.5 us (0.932)
  Pallas kernels: 67.3 us -> 62.8 us
    pallas_call x1, Pallas kernels: 11.9 us -> 7.98 us  [local(): pl.pallas_call(analyse, out_shape=(jax.ShapeDtypeStruct((BLK * M, M), F32...]
where the time goes in v3:
time: 63.5 us; the launch traced here: 63.4 us
  Pallas kernels  62.8 us (99%)
  between operations  0.64 us (1%)
    pallas_call x1, Pallas kernels, local(): pl.pallas_call(observe, out_shape=(pltpu.VMEM((M, M), F32), pltpu.VMEM((B...  54.8 us
    pallas_call x1, Pallas kernels, local(): pl.pallas_call(analyse, out_shape=(jax.ShapeDtypeStruct((BLK * M, M), F32...  7.98 us

profile of v3, /device:TPU:1, one launch (start us, length us, event | category | flops | bytes accessed | tf_op | source)
XLA Modules:
  0.0 63.4 jit_solution(997536958409336696)
XLA Ops:
  0.6 54.8 %observe.1 = (f32[128,128]{1,0:T(8,128)S(1)}, f32[16,128,128]{2,1,0:T(8,128)S(1)}, bf16[128,128,128]{2,1,0:T(8,128)(2,1)S(1)}) custom-call(bf16[128,128,128]{2,1,0:T(8,128)(2,1)} %bitcast.8, bf16[16,4,128,128]{3,2,1,0:T(8,128)(2,1)} %op_hbm.1, s32[4,16]{1,0:T(4,128)} %bitcast.11, f32[16,128]{1,0:T(8,128)} %bitcast.9, f32[16,128]{1,0:T(8,128)} %bitcast.10), custom_call_target="tpu_custom_call" | custom-call | tf_op jit(solution)/shard_map/observe/pallas_call | solution.py:347
  55.4 8.0 %analyse.1 = (f32[2048,128]{1,0:T(8,128)}, bf16[16384,128]{1,0:T(8,128)(2,1)}) custom-call(f32[128,128]{1,0:T(8,128)S(1)} %get-tuple-element.5.gram, f32[2048,128]{1,0:T(8,128)S(1)} %bitcast.7, bf16[16384,128]{1,0:T(8,128)(2,1)S(1)} %bitcast.6), custom_call_target="tpu_custom_call" | custom-call | tf_op jit(solution)/shard_map/analyse/pallas_call | solution.py:402

commit v4 on v3

--- a/solution.py
+++ b/solution.py
@@ -18,7 +18,7 @@
 BAND = 4
 CHUNK = 1
 CHUNKS = BLK // CHUNK
-HALF = CHUNKS // 2
+LEAD = 2
 NEAR = 8
 FAR = 16
 ROWS = M // NEAR
@@ -144,11 +144,13 @@
         serve(3, c)
         return carry
 
+    def serve_far(c, carry):
+        serve(2, c)
+        return carry
+
     def serve_all(c, carry):
         serve(2, c)
-        serve(2, c + HALF)
-        serve_sides(c + HALF, 0)
-        return carry
+        return serve_sides(c, carry)
 
     def to_scalar(e):
         return pltpu.make_async_copy(idx_in.at[BAND - e], idx.at[BAND - e], idx_sem.at[e])
@@ -158,11 +160,12 @@
         to_scalar(e).start()
     for e in (1, 3):
         to_scalar(e).wait()
-    lax.fori_loop(0, HALF, serve_sides, 0)
+    lax.fori_loop(0, LEAD, serve_sides, 0)
     idx_copy(2).wait_recv()
     to_scalar(2).start()
     to_scalar(2).wait()
-    lax.fori_loop(0, HALF, serve_all, 0)
+    lax.fori_loop(0, LEAD, serve_far, 0)
+    lax.fori_loop(LEAD, CHUNKS, serve_all, 0)
     own_idx.wait()
     load_std.wait()
     load_corr.wait()

time: 63.5 us -> 60.1 us (0.946)
  Pallas kernels: 62.8 us -> 59.4 us
    pallas_call x1, Pallas kernels: 54.8 us -> 51.4 us  [local(): pl.pallas_call(observe, out_shape=(pltpu.VMEM((M, M), F32), pltpu.VMEM((B...]
where the time goes in v4:
time: 60.1 us; the launch traced here: 60 us
  Pallas kernels  59.4 us (99%)
  between operations  0.64 us (1%)
    pallas_call x1, Pallas kernels, local(): pl.pallas_call(observe, out_shape=(pltpu.VMEM((M, M), F32), pltpu.VMEM((B...  51.4 us
    pallas_call x1, Pallas kernels, local(): pl.pallas_call(analyse, out_shape=(jax.ShapeDtypeStruct((BLK * M, M), F32...  7.98 us

profile of v4, /device:TPU:1, one launch (start us, length us, event | category | flops | bytes accessed | tf_op | source)
XLA Modules:
  0.0 60.0 jit_solution(15884348834622771893)
XLA Ops:
  0.6 51.4 %observe.1 = (f32[128,128]{1,0:T(8,128)S(1)}, f32[16,128,128]{2,1,0:T(8,128)S(1)}, bf16[128,128,128]{2,1,0:T(8,128)(2,1)S(1)}) custom-call(bf16[128,128,128]{2,1,0:T(8,128)(2,1)} %bitcast.8, bf16[16,4,128,128]{3,2,1,0:T(8,128)(2,1)} %op_hbm.1, s32[4,16]{1,0:T(4,128)} %bitcast.11, f32[16,128]{1,0:T(8,128)} %bitcast.9, f32[16,128]{1,0:T(8,128)} %bitcast.10), custom_call_target="tpu_custom_call" | custom-call | tf_op jit(solution)/shard_map/observe/pallas_call | solution.py:350
  52.0 8.0 %analyse.1 = (f32[2048,128]{1,0:T(8,128)}, bf16[16384,128]{1,0:T(8,128)(2,1)}) custom-call(f32[128,128]{1,0:T(8,128)S(1)} %get-tuple-element.5.gram, f32[2048,128]{1,0:T(8,128)S(1)} %bitcast.7, bf16[16384,128]{1,0:T(8,128)(2,1)S(1)} %bitcast.6), custom_call_target="tpu_custom_call" | custom-call | tf_op jit(solution)/shard_map/analyse/pallas_call | solution.py:405

commit v5 on v4

--- a/solution.py
+++ b/solution.py
@@ -44,7 +44,7 @@
     return jnp.broadcast_to(row, (M, M)).T
 
 
-def combine(n, me, rows_at, parts, left, right, whole):
+def combine(n, me, rows_at, parts, left, right):
     carry = jnp.zeros((1, M), F32)
     product = jnp.ones((1, M), F32)
     cross = jnp.zeros((1, M), F32)
@@ -67,8 +67,8 @@
         square = square + product * product * s
         carry = b + a * carry
         product = product * a
-    whole[...] = jnp.dot(left[...].T, right[...], precision=HIGHEST, preferred_element_type=F32)
-    rows = rows + whole[pl.ds(pl.multiple_of(rows_at, ROWS), ROWS), :]
+    own = pltpu.roll(left[...], (M - rows_at) % M, 1)[:, 0:ROWS]
+    rows = rows + jnp.dot(own.T, right[...], precision=HIGHEST, preferred_element_type=F32)
     state = jnp.concatenate([product, carry, cross, square, jnp.zeros((4, M), F32)], axis=0)
     return rows, state, own_carry, own_product
 
@@ -76,7 +76,7 @@
 def observe(
     anom_hbm, op_hbm, idx_hbm, std_hbm, corr_hbm,
     gram_out, whit, anom,
-    op, idx_vm, std_vm, corr_vm, idx_own, idx_in, idx, send, recv, prod, gram, msg1, in1, msg2, in2, l1, r1, l2, r2, whole, gram_in,
+    op, idx_vm, std_vm, corr_vm, idx_own, idx_in, idx, send, recv, prod, gram, msg1, in1, msg2, in2, l1, r1, l2, r2, gram_in,
     load_sem, idx_sem, idx_send, idx_recv, tile_send, tile_recv, s1, q1, s2, q2, s3, q3,
 ):
     region, band = lax.axis_index("region"), lax.axis_index("band")
@@ -89,25 +89,25 @@
     load_std = pltpu.make_async_copy(std_hbm, std_vm, load_sem.at[3])
     load_corr = pltpu.make_async_copy(corr_hbm, corr_vm, load_sem.at[4])
     load_idx.start()
+
+    def near_peer(e):
+        p = (near + e) % NEAR
+        return (column * 2 + p // BAND, p % BAND), p
+
+    def far_peer(e):
+        q = (column + e) % FAR
+        return (q * 2 + core, band), q
+
+    barrier = pltpu.get_barrier_semaphore()
+    for e in range(1, NEAR):
+        pl.semaphore_signal(barrier, inc=1, device_id=near_peer(e)[0], device_id_type=MESH)
+    for e in range(1, FAR):
+        pl.semaphore_signal(barrier, inc=1, device_id=far_peer(e)[0], device_id_type=MESH)
+
     load_anom.start()
     load_std.start()
     load_corr.start()
     load_op.start()
-
-    def near_peer(e):
-        p = (near + e) % NEAR
-        return (column * 2 + p // BAND, p % BAND), p
-
-    def far_peer(e):
-        q = (column + e) % FAR
-        return (q * 2 + core, band), q
-
-    barrier = pltpu.get_barrier_semaphore()
-    for e in range(1, NEAR):
-        pl.semaphore_signal(barrier, inc=1, device_id=near_peer(e)[0], device_id_type=MESH)
-    for e in range(1, FAR):
-        pl.semaphore_signal(barrier, inc=1, device_id=far_peer(e)[0], device_id_type=MESH)
-
     load_idx.wait()
     idx_own[...] = jnp.zeros((8, M), jnp.int32)
     idx_own[0:BAND, 0:BLK] = idx_vm[...]
@@ -139,6 +139,12 @@
             send[k - 1, j] = anom[idx[BAND - k, k, j]]
         tile_copy(k, c).start()
 
+    def serve_first(k, c):
+        for t in range(CHUNK):
+            j = c * CHUNK + t
+            send[k - 1, j] = anom[idx_in[BAND - k, k : k + 1, :][0, j]]
+        tile_copy(k, c).start()
+
     def serve_sides(c, carry):
         serve(1, c)
         serve(3, c)
@@ -158,9 +164,11 @@
     for e in (1, 3):
         idx_copy(e).wait_recv()
         to_scalar(e).start()
+    for c in range(LEAD):
+        for k in (1, 3):
+            serve_first(k, c)
     for e in (1, 3):
         to_scalar(e).wait()
-    lax.fori_loop(0, LEAD, serve_sides, 0)
     idx_copy(2).wait_recv()
     to_scalar(2).start()
     to_scalar(2).wait()
@@ -211,9 +219,18 @@
     for e in range(1, NEAR):
         copy1(e).start()
     in1[near] = msg1[near]
+
+    def drain(c, carry):
+        for k in range(1, BAND):
+            tile_copy(k, c).wait_send()
+        return carry
+
+    lax.fori_loop(0, CHUNKS, drain, 0)
+    for e in (2, 1, 3):
+        idx_copy(e).wait_send()
     for e in range(1, NEAR):
         copy1(e).wait_recv()
-    rows, state, own_carry, own_product = combine(NEAR, near, near * ROWS, in1, l1, r1, whole)
+    rows, state, own_carry, own_product = combine(NEAR, near, near * ROWS, in1, l1, r1)
     msg2[0:ROWS] = rows
     msg2[ROWS : ROWS + 8] = state
 
@@ -227,9 +244,11 @@
     for e in range(1, FAR):
         copy2(e).start()
     in2[column] = msg2[...]
+    for e in range(1, NEAR):
+        copy1(e).wait_send()
     for e in range(1, FAR):
         copy2(e).wait_recv()
-    rows, state, far_carry, _ = combine(FAR, column, near * ROWS, in2, l2, r2, whole)
+    rows, state, far_carry, _ = combine(FAR, column, near * ROWS, in2, l2, r2)
     here = lax.broadcasted_iota(jnp.int32, (ROWS, M), 0) + near * ROWS
     lane = lax.broadcasted_iota(jnp.int32, (ROWS, M), 1)
     rows = rows + jnp.where(here == lane, M - 1.0, 0.0)
@@ -253,24 +272,14 @@
         return carry
 
     lax.fori_loop(0, BLK, settle, 0)
+    for e in range(1, FAR):
+        copy2(e).wait_send()
     for e in range(1, NEAR):
         copy3(e).wait_recv()
     gram_out[...] = gram_in[...]
 
-    for e in (2, 1, 3):
-        idx_copy(e).wait_send()
-
-    def drain(c, carry):
-        for k in range(1, BAND):
-            tile_copy(k, c).wait_send()
-        return carry
-
-    lax.fori_loop(0, CHUNKS, drain, 0)
-    for e in range(1, NEAR):
-        copy1(e).wait_send()
+    for e in range(1, NEAR):
         copy3(e).wait_send()
-    for e in range(1, FAR):
-        copy2(e).wait_send()
 
 
 def inverse_factor(work, gram):
@@ -278,12 +287,11 @@
     lane = lax.broadcasted_iota(jnp.int32, (8, M), 1)
     sub = lax.broadcasted_iota(jnp.int32, (8, M), 0)
     rows = [gram[8 * i : 8 * i + 8, :] for i in range(n)]
-    done = []
     for p in range(n):
         base = 8 * p
         block = rows[p]
         cols = [jnp.broadcast_to(block[:, base + l : base + l + 1], (8, M)) for l in range(8)]
-        s = [[jnp.broadcast_to(cols[l][j : j + 1, :], (8, M)) for l in range(8)] for j in range(8)]
+        s = {(j, l): jnp.broadcast_to(cols[l][j : j + 1, :], (8, M)) for l in range(8) for j in range(l + 1)}
         inside = (lane >= base) & (lane < base + 8)
         r = []
         for j in range(8):
@@ -291,37 +299,33 @@
             r.append(jnp.where(inside, jnp.where(lane == base + j, 1.0, 0.0), own))
         lower, pivot = [], []
         for j in range(8):
-            inv = 1.0 / s[j][j]
+            inv = 1.0 / s[j, j]
             lower.append(r[j])
-            pivot.append(s[j][j])
+            pivot.append(s[j, j])
             for i in range(8):
                 if i == j:
                     continue
-                f = s[i][j] * inv
-                for l in range(j + 1, 8):
-                    s[i][l] = s[i][l] - f * s[j][l]
+                f = (s[j, i] if i > j else s[i, j]) * inv
+                for l in range(max(i, j + 1), 8):
+                    s[i, l] = s[i, l] - f * s[j, l]
                 r[i] = r[i] - f * r[j]
             for l in range(j + 1, 8):
-                s[j][l] = s[j][l] * inv
+                s[j, l] = s[j, l] * inv
             r[j] = r[j] * inv
-            s[j][j] = None
-        out = lower[0]
-        d = pivot[0]
+        out, d = lower[0], pivot[0]
         for j in range(1, 8):
             out = jnp.where(sub == j, lower[j], out)
             d = jnp.where(sub == j, pivot[j], d)
         keep = lane <= base + sub
-        done.append(jnp.where(keep, out * lax.rsqrt(d), 0.0))
+        work[8 * p : 8 * p + 8, :] = jnp.where(keep, out * lax.rsqrt(d), 0.0)
         for i in range(p + 1, n):
             t = jnp.where(inside, 0.0, rows[i])
             for l in range(8):
                 t = t - jnp.broadcast_to(rows[i][:, base + l : base + l + 1], (8, M)) * r[l]
             rows[i] = t
-    for p in range(n):
-        work[8 * p : 8 * p + 8, :] = done[p]
-
-
-PIECES = 8
+
+
+PIECES = 16
 PIECE = 128 * M // PIECES
 
 
@@ -376,7 +380,6 @@
             pltpu.VMEM((2 * NEAR, M), F32),
             pltpu.VMEM((2 * FAR, M), F32),
             pltpu.VMEM((2 * FAR, M), F32),
-            pltpu.VMEM((M, M), F32),
             pltpu.VMEM((M, M), F32),
             dma((5,)),
             dma((BAND,)),

time: 60.1 us -> 59.1 us (0.983)
  Pallas kernels: 59.4 us -> 58.3 us
    pallas_call x1, Pallas kernels: 51.4 us -> 50.7 us  [local(): pl.pallas_call(observe, out_shape=(pltpu.VMEM((M, M), F32), pltpu.VMEM((B...]
where the time goes in v5:
time: 59.1 us; the launch traced here: 59 us
  Pallas kernels  58.3 us (99%)
  between operations  0.64 us (1%)
    pallas_call x1, Pallas kernels, local(): pl.pallas_call(observe, out_shape=(pltpu.VMEM((M, M), F32), pltpu.VMEM((B...  50.7 us
    pallas_call x1, Pallas kernels, local(): pl.pallas_call(analyse, out_shape=(jax.ShapeDtypeStruct((BLK * M, M), F32...  7.58 us

profile of v5, /device:TPU:1, one launch (start us, length us, event | category | flops | bytes accessed | tf_op | source)
XLA Modules:
  0.0 59.0 jit_solution(18315250094638383735)
XLA Ops:
  0.6 50.7 %observe.1 = (f32[128,128]{1,0:T(8,128)S(1)}, f32[16,128,128]{2,1,0:T(8,128)S(1)}, bf16[128,128,128]{2,1,0:T(8,128)(2,1)S(1)}) custom-call(bf16[128,128,128]{2,1,0:T(8,128)(2,1)} %bitcast.8, bf16[16,4,128,128]{3,2,1,0:T(8,128)(2,1)} %op_hbm.1, s32[4,16]{1,0:T(4,128)} %bitcast.11, f32[16,128]{1,0:T(8,128)} %bitcast.9, f32[16,128]{1,0:T(8,128)} %bitcast.10), custom_call_target="tpu_custom_call" | custom-call | tf_op jit(solution)/shard_map/observe/pallas_call | solution.py:354
  51.4 7.6 %analyse.1 = (f32[2048,128]{1,0:T(8,128)}, bf16[16384,128]{1,0:T(8,128)(2,1)}) custom-call(f32[128,128]{1,0:T(8,128)S(1)} %get-tuple-element.5.gram, f32[2048,128]{1,0:T(8,128)S(1)} %bitcast.7, bf16[16384,128]{1,0:T(8,128)(2,1)S(1)} %bitcast.6), custom_call_target="tpu_custom_call" | custom-call | tf_op jit(solution)/shard_map/analyse/pallas_call | solution.py:408

commit v6 on v5

--- a/solution.py
+++ b/solution.py
@@ -21,6 +21,8 @@
 LEAD = 2
 NEAR = 8
 FAR = 16
+NEAR_ORDER = (6, 2, 5, 7, 1, 3, 4)
+FAR_ORDER = (10, 6, 9, 11, 14, 2, 5, 7, 8, 13, 15, 1, 3, 4, 12)
 ROWS = M // NEAR
 OBSERVE_VMEM = 52 * 1024 * 1024
 ANALYSE_VMEM = 16 * 1024 * 1024
@@ -53,7 +55,7 @@
     rows = jnp.zeros((ROWS, M), F32)
     for i in range(n):
         rows = rows + parts[i, 0:ROWS]
-        state = parts[i, ROWS : ROWS + 8]
+        state = parts[i, ROWS : ROWS + 4]
         a, b, h, s = (state[k : k + 1] for k in range(4))
         mine = me == i
         own_carry = jnp.where(mine, carry, own_carry)
@@ -69,7 +71,7 @@
         product = product * a
     own = pltpu.roll(left[...], (M - rows_at) % M, 1)[:, 0:ROWS]
     rows = rows + jnp.dot(own.T, right[...], precision=HIGHEST, preferred_element_type=F32)
-    state = jnp.concatenate([product, carry, cross, square, jnp.zeros((4, M), F32)], axis=0)
+    state = jnp.concatenate([product, carry, cross, square], axis=0)
     return rows, state, own_carry, own_product
 
 
@@ -91,11 +93,11 @@
     load_idx.start()
 
     def near_peer(e):
-        p = (near + e) % NEAR
+        p = (core + e // BAND) % 2 * BAND + (band + e % BAND) % BAND
         return (column * 2 + p // BAND, p % BAND), p
 
     def far_peer(e):
-        q = (column + e) % FAR
+        q = (column // 4 + e // 4) % 4 * 4 + (column % 4 + e % 4) % 4
         return (q * 2 + core, band), q
 
     barrier = pltpu.get_barrier_semaphore()
@@ -204,10 +206,10 @@
     zero = jnp.zeros((1, M), F32)
     last, product, cross, square = lax.fori_loop(0, CHUNKS, use, (zero, jnp.ones((1, M), F32), zero, zero))
 
-    state = jnp.concatenate([product, last, cross, square, jnp.zeros((4, M), F32)], axis=0)
+    state = jnp.concatenate([product, last, cross, square], axis=0)
     for p in range(NEAR):
         msg1[p, 0:ROWS] = gram[p * ROWS : (p + 1) * ROWS]
-        msg1[p, ROWS : ROWS + 8] = state
+        msg1[p, ROWS : ROWS + 4] = state
 
     def copy1(e):
         device, p = near_peer(e)
@@ -216,7 +218,7 @@
             device_id=device, device_id_type=MESH,
         )
 
-    for e in range(1, NEAR):
+    for e in NEAR_ORDER:
         copy1(e).start()
     in1[near] = msg1[near]
 
@@ -232,7 +234,7 @@
         copy1(e).wait_recv()
     rows, state, own_carry, own_product = combine(NEAR, near, near * ROWS, in1, l1, r1)
     msg2[0:ROWS] = rows
-    msg2[ROWS : ROWS + 8] = state
+    msg2[ROWS : ROWS + 4] = state
 
     def copy2(e):
         device, _ = far_peer(e)
@@ -241,7 +243,7 @@
             device_id=device, device_id_type=MESH,
         )
 
-    for e in range(1, FAR):
+    for e in FAR_ORDER:
         copy2(e).start()
     in2[column] = msg2[...]
     for e in range(1, NEAR):
@@ -262,7 +264,7 @@
             device_id=device, device_id_type=MESH,
         )
 
-    for e in range(1, NEAR):
+    for e in NEAR_ORDER:
         copy3(e).start()
 
     before = own_carry + own_product * far_carry
@@ -282,7 +284,7 @@
         copy3(e).wait_send()
 
 
-def inverse_factor(work, gram):
+def inverse_factor(work, gram, spread):
     n = M // 8
     lane = lax.broadcasted_iota(jnp.int32, (8, M), 1)
     sub = lax.broadcasted_iota(jnp.int32, (8, M), 0)
@@ -291,7 +293,14 @@
         base = 8 * p
         block = rows[p]
         cols = [jnp.broadcast_to(block[:, base + l : base + l + 1], (8, M)) for l in range(8)]
-        s = {(j, l): jnp.broadcast_to(cols[l][j : j + 1, :], (8, M)) for l in range(8) for j in range(l + 1)}
+        side = p % 2 * 64
+        for l in range(8):
+            spread[side + 8 * l : side + 8 * l + 8, :] = cols[l]
+        s = {}
+        for l in range(8):
+            for j in range(l + 1):
+                at = side + 8 * l + j
+                s[j, l] = jnp.broadcast_to(spread[at : at + 1, :], (8, M))
         inside = (lane >= base) & (lane < base + 8)
         r = []
         for j in range(8):
@@ -329,14 +338,14 @@
 PIECE = 128 * M // PIECES
 
 
-def analyse(gram, whit, anom, whit_out, out_hbm, out, work, out_sem, whit_sem):
+def analyse(gram, whit, anom, whit_out, out_hbm, out, work, spread, out_sem, whit_sem):
     def store(i):
         at = pl.ds(i * PIECE, PIECE)
         return pltpu.make_async_copy(out.at[at], out_hbm.at[at], out_sem.at[i])
 
     store_whit = pltpu.make_async_copy(whit, whit_out, whit_sem)
     store_whit.start()
-    inverse_factor(work, gram[...])
+    inverse_factor(work, gram[...], spread)
     transform = (math.sqrt(M - 1.0) * work[...].T).astype(BF16)
     for i in range(PIECES):
         at = pl.ds(i * PIECE, PIECE)
@@ -372,10 +381,10 @@
             pltpu.VMEM((BAND - 1, BLK, M, M), BF16),
             pltpu.VMEM((BLK, M, M), F32),
             pltpu.VMEM((M, M), F32),
-            pltpu.VMEM((NEAR, ROWS + 8, M), F32),
-            pltpu.VMEM((NEAR, ROWS + 8, M), F32),
-            pltpu.VMEM((ROWS + 8, M), F32),
-            pltpu.VMEM((FAR, ROWS + 8, M), F32),
+            pltpu.VMEM((NEAR, ROWS + 4, M), F32),
+            pltpu.VMEM((NEAR, ROWS + 4, M), F32),
+            pltpu.VMEM((ROWS + 4, M), F32),
+            pltpu.VMEM((FAR, ROWS + 4, M), F32),
             pltpu.VMEM((2 * NEAR, M), F32),
             pltpu.VMEM((2 * NEAR, M), F32),
             pltpu.VMEM((2 * FAR, M), F32),
@@ -413,6 +422,7 @@
         scratch_shapes=[
             pltpu.VMEM((M * M, M), BF16),
             pltpu.VMEM((M, M), F32),
+            pltpu.VMEM((2 * 64, M), F32),
             dma((PIECES,)),
             dma,
         ],

time: 59.1 us -> 57.4 us (0.971)
  Pallas kernels: 58.3 us -> 56.7 us
    pallas_call x1, Pallas kernels: 7.58 us -> 6.5 us  [local(): pl.pallas_call(analyse, out_shape=(jax.ShapeDtypeStruct((BLK * M, M), F32...]
where the time goes in v6:
time: 57.4 us; the launch traced here: 57.3 us
  Pallas kernels  56.7 us (99%)
  between operations  0.64 us (1%)
    pallas_call x1, Pallas kernels, local(): pl.pallas_call(observe, out_shape=(pltpu.VMEM((M, M), F32), pltpu.VMEM((B...  50.2 us
    pallas_call x1, Pallas kernels, local(): pl.pallas_call(analyse, out_shape=(jax.ShapeDtypeStruct((BLK * M, M), F32...  6.5 us

profile of v6, /device:TPU:1, one launch (start us, length us, event | category | flops | bytes accessed | tf_op | source)
XLA Modules:
  0.0 57.3 jit_solution(17029372840086850526)
XLA Ops:
  0.6 50.2 %observe.1 = (f32[128,128]{1,0:T(8,128)S(1)}, f32[16,128,128]{2,1,0:T(8,128)S(1)}, bf16[128,128,128]{2,1,0:T(8,128)(2,1)S(1)}) custom-call(bf16[128,128,128]{2,1,0:T(8,128)(2,1)} %bitcast.8, bf16[16,4,128,128]{3,2,1,0:T(8,128)(2,1)} %op_hbm.1, s32[4,16]{1,0:T(4,128)} %bitcast.11, f32[16,128]{1,0:T(8,128)} %bitcast.9, f32[16,128]{1,0:T(8,128)} %bitcast.10), custom_call_target="tpu_custom_call" | custom-call | tf_op jit(solution)/shard_map/observe/pallas_call | solution.py:363
  50.8 6.5 %analyse.1 = (f32[2048,128]{1,0:T(8,128)}, bf16[16384,128]{1,0:T(8,128)(2,1)}) custom-call(f32[128,128]{1,0:T(8,128)S(1)} %get-tuple-element.5.gram, f32[2048,128]{1,0:T(8,128)S(1)} %bitcast.7, bf16[16384,128]{1,0:T(8,128)(2,1)S(1)} %bitcast.6), custom_call_target="tpu_custom_call" | custom-call | tf_op jit(solution)/shard_map/analyse/pallas_call | solution.py:417

commit v7 on v6

--- a/solution.py
+++ b/solution.py
@@ -152,10 +152,6 @@
         serve(3, c)
         return carry
 
-    def serve_far(c, carry):
-        serve(2, c)
-        return carry
-
     def serve_all(c, carry):
         serve(2, c)
         return serve_sides(c, carry)
@@ -173,8 +169,9 @@
         to_scalar(e).wait()
     idx_copy(2).wait_recv()
     to_scalar(2).start()
+    for c in range(LEAD):
+        serve_first(2, c)
     to_scalar(2).wait()
-    lax.fori_loop(0, LEAD, serve_far, 0)
     lax.fori_loop(LEAD, CHUNKS, serve_all, 0)
     own_idx.wait()
     load_std.wait()
@@ -328,10 +325,10 @@
         keep = lane <= base + sub
         work[8 * p : 8 * p + 8, :] = jnp.where(keep, out * lax.rsqrt(d), 0.0)
         for i in range(p + 1, n):
-            t = jnp.where(inside, 0.0, rows[i])
-            for l in range(8):
-                t = t - jnp.broadcast_to(rows[i][:, base + l : base + l + 1], (8, M)) * r[l]
-            rows[i] = t
+            terms = [jnp.broadcast_to(rows[i][:, base + l : base + l + 1], (8, M)) * r[l] for l in range(8)]
+            while len(terms) > 1:
+                terms = [a + b for a, b in zip(terms[0::2], terms[1::2])]
+            rows[i] = jnp.where(inside, 0.0, rows[i]) - terms[0]
 
 
 PIECES = 16

time: 57.4 us -> 57 us (level)
  no operation moved by 1% of the time
where the time goes in v7:
time: 57 us; the launch traced here: 56.9 us
  Pallas kernels  56.2 us (99%)
  between operations  0.64 us (1%)
    pallas_call x1, Pallas kernels, local(): pl.pallas_call(observe, out_shape=(pltpu.VMEM((M, M), F32), pltpu.VMEM((B...  49.8 us
    pallas_call x1, Pallas kernels, local(): pl.pallas_call(analyse, out_shape=(jax.ShapeDtypeStruct((BLK * M, M), F32...  6.45 us

profile of v7, /device:TPU:1, one launch (start us, length us, event | category | flops | bytes accessed | tf_op | source)
XLA Modules:
  0.0 56.9 jit_solution(2672954125874143598)
XLA Ops:
  0.6 49.8 %observe.1 = (f32[128,128]{1,0:T(8,128)S(1)}, f32[16,128,128]{2,1,0:T(8,128)S(1)}, bf16[128,128,128]{2,1,0:T(8,128)(2,1)S(1)}) custom-call(bf16[128,128,128]{2,1,0:T(8,128)(2,1)} %bitcast.8, bf16[16,4,128,128]{3,2,1,0:T(8,128)(2,1)} %op_hbm.1, s32[4,16]{1,0:T(4,128)} %bitcast.11, f32[16,128]{1,0:T(8,128)} %bitcast.9, f32[16,128]{1,0:T(8,128)} %bitcast.10), custom_call_target="tpu_custom_call" | custom-call | tf_op jit(solution)/shard_map/observe/pallas_call | solution.py:360
  50.4 6.4 %analyse.1 = (f32[2048,128]{1,0:T(8,128)}, bf16[16384,128]{1,0:T(8,128)(2,1)}) custom-call(f32[128,128]{1,0:T(8,128)S(1)} %get-tuple-element.5.gram, f32[2048,128]{1,0:T(8,128)S(1)} %bitcast.7, bf16[16384,128]{1,0:T(8,128)(2,1)S(1)} %bitcast.6), custom_call_target="tpu_custom_call" | custom-call | tf_op jit(solution)/shard_map/analyse/pallas_call | solution.py:414

commit v8 on v7

--- a/solution.py
+++ b/solution.py
@@ -162,9 +162,8 @@
     for e in (1, 3):
         idx_copy(e).wait_recv()
         to_scalar(e).start()
-    for c in range(LEAD):
-        for k in (1, 3):
-            serve_first(k, c)
+        for c in range(LEAD):
+            serve_first(e, c)
     for e in (1, 3):
         to_scalar(e).wait()
     idx_copy(2).wait_recv()

time: 57 us -> 57.2 us (level)
  no operation moved by 1% of the time
where the time goes in v8:
time: 57.2 us; the launch traced here: 57.1 us
  Pallas kernels  56.4 us (99%)
  between operations  0.64 us (1%)
    pallas_call x1, Pallas kernels, local(): pl.pallas_call(observe, out_shape=(pltpu.VMEM((M, M), F32), pltpu.VMEM((B...  50 us
    pallas_call x1, Pallas kernels, local(): pl.pallas_call(analyse, out_shape=(jax.ShapeDtypeStruct((BLK * M, M), F32...  6.45 us

profile of v8, /device:TPU:1, one launch (start us, length us, event | category | flops | bytes accessed | tf_op | source)
XLA Modules:
  0.0 57.1 jit_solution(430101838130393351)
XLA Ops:
  0.6 50.0 %observe.1 = (f32[128,128]{1,0:T(8,128)S(1)}, f32[16,128,128]{2,1,0:T(8,128)S(1)}, bf16[128,128,128]{2,1,0:T(8,128)(2,1)S(1)}) custom-call(bf16[128,128,128]{2,1,0:T(8,128)(2,1)} %bitcast.8, bf16[16,4,128,128]{3,2,1,0:T(8,128)(2,1)} %op_hbm.1, s32[4,16]{1,0:T(4,128)} %bitcast.11, f32[16,128]{1,0:T(8,128)} %bitcast.9, f32[16,128]{1,0:T(8,128)} %bitcast.10), custom_call_target="tpu_custom_call" | custom-call | tf_op jit(solution)/shard_map/observe/pallas_call | solution.py:359
  50.6 6.4 %analyse.1 = (f32[2048,128]{1,0:T(8,128)}, bf16[16384,128]{1,0:T(8,128)(2,1)}) custom-call(f32[128,128]{1,0:T(8,128)S(1)} %get-tuple-element.5.gram, f32[2048,128]{1,0:T(8,128)S(1)} %bitcast.7, bf16[16384,128]{1,0:T(8,128)(2,1)S(1)} %bitcast.6), custom_call_target="tpu_custom_call" | custom-call | tf_op jit(solution)/shard_map/analyse/pallas_call | solution.py:413

commit v9 on v7

--- a/solution.py
+++ b/solution.py
@@ -341,8 +341,8 @@
         return pltpu.make_async_copy(out.at[at], out_hbm.at[at], out_sem.at[i])
 
     store_whit = pltpu.make_async_copy(whit, whit_out, whit_sem)
+    inverse_factor(work, gram[...], spread)
     store_whit.start()
-    inverse_factor(work, gram[...], spread)
     transform = (math.sqrt(M - 1.0) * work[...].T).astype(BF16)
     for i in range(PIECES):
         at = pl.ds(i * PIECE, PIECE)

time: 57 us -> 57 us (level)
  no operation moved by 1% of the time
where the time goes in v9:
time: 57 us; the launch traced here: 56.9 us
  Pallas kernels  56.2 us (99%)
  between operations  0.64 us (1%)
    pallas_call x1, Pallas kernels, local(): pl.pallas_call(observe, out_shape=(pltpu.VMEM((M, M), F32), pltpu.VMEM((B...  49.8 us
    pallas_call x1, Pallas kernels, local(): pl.pallas_call(analyse, out_shape=(jax.ShapeDtypeStruct((BLK * M, M), F32...  6.45 us

profile of v9, /device:TPU:1, one launch (start us, length us, event | category | flops | bytes accessed | tf_op | source)
XLA Modules:
  0.0 56.9 jit_solution(2672954125874143598)
XLA Ops:
  0.6 49.8 %observe.1 = (f32[128,128]{1,0:T(8,128)S(1)}, f32[16,128,128]{2,1,0:T(8,128)S(1)}, bf16[128,128,128]{2,1,0:T(8,128)(2,1)S(1)}) custom-call(bf16[128,128,128]{2,1,0:T(8,128)(2,1)} %bitcast.8, bf16[16,4,128,128]{3,2,1,0:T(8,128)(2,1)} %op_hbm.1, s32[4,16]{1,0:T(4,128)} %bitcast.11, f32[16,128]{1,0:T(8,128)} %bitcast.9, f32[16,128]{1,0:T(8,128)} %bitcast.10), custom_call_target="tpu_custom_call" | custom-call | tf_op jit(solution)/shard_map/observe/pallas_call | solution.py:360
  50.4 6.4 %analyse.1 = (f32[2048,128]{1,0:T(8,128)}, bf16[16384,128]{1,0:T(8,128)(2,1)}) custom-call(f32[128,128]{1,0:T(8,128)S(1)} %get-tuple-element.5.gram, f32[2048,128]{1,0:T(8,128)S(1)} %bitcast.7, bf16[16384,128]{1,0:T(8,128)(2,1)S(1)} %bitcast.6), custom_call_target="tpu_custom_call" | custom-call | tf_op jit(solution)/shard_map/analyse/pallas_call | solution.py:414
